TPU v7x, 32 devices: a whole 2x2x4 slice. The times are simulated.
32 devices in a mesh: row: 4 (over y, x), col: 8 (over z, core).
Axes of the slice: x: 2, y: 2, z: 4, core: 2. Of those that a mesh axis runs over, the one named last changes fastest.
Arguments:
- sigma_anc: bfloat16 [1024, 1024], P('row', 'col'), as said below
- structure: int32 [32, 4], P(('row', 'col')), may hold values from 0 to 3, all different within a row
- factor: bfloat16 [32, 1024, 1024], P(('row', 'col')), may hold values from -0.375 to 0.375
- diag_term: float32 [32, 1024], P(('row', 'col')), may hold values from 1 to 8
Outputs:
- sigma_off: bfloat16 [32, 1024, 1024], P(('row', 'col'))
- variances: float32 [32, 1024], P(('row', 'col'))
Inputs may be any that keep to these rules, and one draw needn't show every extreme that they name: `structure`: each row names 4 different ancestor blocks, and every ancestor block is named by some row. sigma_anc is exactly symmetric, as the inverse of a symmetric precision matrix: its entry (p, q) equals its entry (q, p) bit for bit.
All inputs are finite; a program needn't handle non-finite values.
Results may differ from a plain program's by a relative error of at most 0.001.
Values may be sent and summed in bfloat16 or wider, within the bound.
A program may use at most 64 MiB of HBM per device.

v0:
```python
import jax
import jax.numpy as jnp
from jax import lax
from jax.sharding import PartitionSpec as P


def body(sigma_anc, structure, factor, diag_term):
    span_count = structure.shape[1]
    block_rows = factor.shape[1] // span_count
    own_blocks = structure[0]
    triangle = factor[0]
    panel = lax.all_gather(sigma_anc, "col", axis=1, tiled=True)
    structures = lax.all_gather(structure, "row", axis=0, tiled=True)
    block_total = panel.shape[1] // block_rows
    blocked = panel.reshape(block_rows, block_total, block_rows)
    outgoing = jnp.take(blocked, structures, axis=1)
    outgoing = outgoing.reshape(block_rows, structures.shape[0], span_count * block_rows)
    received = lax.all_to_all(outgoing, "row", split_axis=1, concat_axis=1, tiled=True)
    picked = jnp.take(received, own_blocks, axis=1)
    product = jnp.einsum("bim,mw->ibw", picked, triangle, preferred_element_type=jnp.float32)
    off_block = -product.reshape(span_count * block_rows, triangle.shape[1])
    variance = diag_term[0] - jnp.sum(triangle.astype(jnp.float32) * off_block, axis=0)
    return (off_block.astype(jnp.bfloat16)[None], variance[None])


def solution(mesh):
    return jax.shard_map(
        body,
        mesh=mesh,
        in_specs=(
            P("row", "col"),
            P(("row", "col"), None),
            P(("row", "col"), None, None),
            P(("row", "col"), None),
        ),
        out_specs=(P(("row", "col"), None, None), P(("row", "col"), None)),
        check_vma=False,
    )
```

profile of v0, /device:TPU:1, one launch (start us, length us, event | category | flops | bytes accessed | tf_op | source)
XLA Modules:
  0.0 67.2 jit_solution(4180997930560623704)
XLA Ops:
  0.6 7.1 %all-gather = s32[4,1,4]{2,1,0:T(1,128)S(1)} all-gather(s32[1,1,4]{2,1,0:T(1,128)} %bitcast.46), channel_id=1, replica_groups=mesh['row'=4,'col'=8] {'row'}, dimensions={0}, use_global_device_ids=true | all-gather | bytes 80 | tf_op jit(solution)/shard_map/all_gather | solution.py:13
  7.8 0.1 reshape.70
  7.9 0.1 broadcast_bitcast_fusion
  7.9 0.9 %copy.10 = bf16[256,128]{0,1:T(8,128)(2,1)S(1)} copy(bf16[256,128]{1,0:T(8,128)(2,1)} %param.4) | data formatting | bytes 131072 | tf_op args[0]
  8.9 17.7 %all_gather.7 = bf16[256,1024]{0,1:T(8,128)(2,1)S(1)} all-gather(bf16[256,128]{0,1:T(8,128)(2,1)S(1)} %copy.10), channel_id=1, replica_groups=mesh['row'=4,'col'=8] {'col'}, dimensions={1}, use_global_device_ids=true | all-gather | bytes 589824 | tf_op jit(solution)/shard_map/all_gather | solution.py:12
  26.6 0.2 copy.11
  26.8 0.7 %gather_fusion = bf16[16,256,256]{2,1,0:T(8,128)(2,1)S(1)} fusion(bf16[256,4,256]{2,0,1:T(8,128)(2,1)S(1)} %copy.11, s32[1024]{0:T(1024)S(1)} %pad_clamp_fusion.1), kind=kCustom, calls=%fused_computation | custom fusion | bytes 4194368 | tf_op jit(solution)/shard_map/jit(_take)/gather | solution.py:16
  27.4 0.3 copy.13
  27.7 1.5 %broadcast_select_fusion = bf16[256,4,1024]{2,0,1:T(8,128)(2,1)} fusion(bf16[256,4,1024]{2,0,1:T(8,128)(2,1)S(1)} %bitcast.39, pred[4,1024]{1,0:T(4,128)(4,1)S(1)} %bitcast.44), kind=kLoop, calls=%fused_computation.9 | loop fusion | flops 1048576 | bytes 4198400 | tf_op jit(solution)/shard_map/jit(_take)/select_n | solution.py:16
  29.3 0.0 copy-start.2
  29.3 3.7 %all-to-all-start = ((bf16[256,4,1024]{2,0,1:T(8,128)(2,1)}), bf16[256,4,1024]{2,0,1:T(8,128)(2,1)S(1)}, u32[]{:S(2)}, u32[]{:S(2)}) async-start(bf16[256,4,1024]{2,0,1:T(8,128)(2,1)} %broadcast_select_fusion), calls=%async_computation | async-start | bytes 4194304 | tf_op jit(solution)/shard_map/all_to_all | solution.py:18
  33.0 0.0 copy-done.2
  33.1 24.8 %all-to-all-done = bf16[256,4,1024]{2,0,1:T(8,128)(2,1)S(1)} async-done(((bf16[256,4,1024]{2,0,1:T(8,128)(2,1)}), bf16[256,4,1024]{2,0,1:T(8,128)(2,1)S(1)}, u32[]{:S(2)}, u32[]{:S(2)}) %all-to-all-start) | async-done | bytes 2097184 | tf_op jit(solution)/shard_map/all_to_all | solution.py:18
  57.8 2.0 %gather_fusion.1 = bf16[4,256,1024]{2,1,0:T(8,128)(2,1)} fusion(bf16[256,4,1024]{2,0,1:T(8,128)(2,1)S(1)} %all-to-all-done, s32[1024]{0:T(1024)S(1)} %pad_clamp_fusion), kind=kCustom, calls=%fused_computation.1 | custom fusion | bytes 4194320 | tf_op jit(solution)/shard_map/jit(_take)/gather | solution.py:19
  59.9 0.0 copy-start
  59.9 6.1 %fusion.8 = (bf16[256,4,1024]{2,0,1:T(8,128)(2,1)}, f32[256,4,1024]{2,0,1:T(8,128)S(1)}) fusion(bf16[1,1024,1024]{2,1,0:T(8,128)(2,1)} %param.6, bf16[4,256,1024]{2,1,0:T(8,128)(2,1)} %gather_fusion.1, pred[4]{0:T(512)(128)(4,1)S(1)} %compare_and_fusion.1), kind=kOutput, calls=%fused_computation.21 | convolution fusion | flops 2150629376 | bytes 10485764 | tf_op jit(solution)/shard_map/bim,mw->ibw/dot_general | solution.py:20
  65.9 0.0 copy-done
  65.9 0.0 copy-start.1
  65.9 0.5 fusion
  66.5 0.1 copy-done.1
  66.6 0.6 sub.4
  (7 shorter events, 0.0 us)
Async XLA Ops:
  29.3 3.8 %copy-start.2 = (s32[1,4]{1,0:T(1,128)S(1)}, s32[1,4]{1,0:T(1,128)}, u32[]{:S(2)}) copy-start(s32[1,4]{1,0:T(1,128)} %param.5) | copy-start | bytes 52
  29.3 28.6 %all-to-all-start = ((bf16[256,4,1024]{2,0,1:T(8,128)(2,1)}), bf16[256,4,1024]{2,0,1:T(8,128)(2,1)S(1)}, u32[]{:S(2)}, u32[]{:S(2)}) async-start(bf16[256,4,1024]{2,0,1:T(8,128)(2,1)} %broadcast_select_fusion), calls=%async_computation | async-start | bytes 4194304 | tf_op jit(solution)/shard_map/all_to_all | solution.py:18
  59.9 6.1 %copy-start = (bf16[1,1024,1024]{2,1,0:T(8,128)(2,1)S(1)}, bf16[1,1024,1024]{2,1,0:T(8,128)(2,1)}, u32[]{:S(2)}) copy-start(bf16[1,1024,1024]{2,1,0:T(8,128)(2,1)} %param.6) | copy-start | bytes 6291460
  65.9 0.7 %copy-start.1 = (f32[1,1024]{1,0:T(1,128)S(1)}, f32[1,1024]{1,0:T(1,128)}, u32[]{:S(2)}) copy-start(f32[1,1024]{1,0:T(1,128)} %param.7) | copy-start | bytes 12292
where the time goes:
time: 68.4 us; the launch traced here: 67.2 us
  blocking collectives  24.8 us (36%)
  waiting for transfers between devices  24.8 us (36%)
  matrix products  6.06 us (9%)
  local copies, waits for them, and re-layouts  4.43 us (6%)
  starting transfers between devices  3.74 us (5%)
  other arithmetic  2.72 us (4%)
  between operations  0.71 us (1%)
    all_to_all x1, waiting for transfers between devices, body(): lax.all_to_all(outgoing, 'row', split_axis=1, concat_axis=1, tiled=True)  24.8 us
    all_gather x1, blocking collectives, body(): panel = lax.all_gather(sigma_anc, 'col', axis=1, tiled=True)  17.7 us
    all_gather x1, blocking collectives, body(): structures = lax.all_gather(structure, 'row', axis=0, tiled=True)  7.11 us
    dot_general x1, matrix products, body(): jnp.einsum('bim,mw->ibw', picked, triangle, preferred_element_type=jnp.fl...  6.06 us
    all_to_all x1, starting transfers between devices, body(): lax.all_to_all(outgoing, 'row', split_axis=1, concat_axis=1, tiled=True)  3.74 us
    gather x1, local copies, waits for them, and re-layouts, body(): picked = jnp.take(received, own_blocks, axis=1)  2.01 us
    select_n x2, other arithmetic, body(): outgoing = jnp.take(blocked, structures, axis=1)  1.54 us
  transfers between devices with their start and end apart: 1, of which 1 were waited for; matrix products, arithmetic and copies ran while one was open for 0% of the time, Pallas kernels for 0%

commit v1 on v0

--- a/solution.py
+++ b/solution.py
@@ -1,10 +1,231 @@
+import functools
+
 import jax
 import jax.numpy as jnp
 from jax import lax
+from jax.experimental import pallas as pl
+from jax.experimental.pallas import tpu as pltpu
 from jax.sharding import PartitionSpec as P
 
-
-def body(sigma_anc, structure, factor, diag_term):
+MESH = pl.DeviceIdType.MESH
+OWN, ALONG_X, ALONG_Y, ACROSS = range(4)
+
+
+def flip(value, mask):
+    bit = 1
+    while bit <= mask:
+        if mask & bit:
+            value = value + bit - 2 * bit * ((value // bit) % 2)
+        bit *= 2
+    return value
+
+
+def kernel(
+    planes,
+    sigma_ref,
+    structure_ref,
+    factor_ref,
+    diag_ref,
+    out_ref,
+    var_ref,
+    held,
+    gram,
+    tri,
+    result,
+    local_sem,
+    out_sem,
+    line_send,
+    line_recv,
+    pair_send,
+    pair_recv,
+    core_send,
+    core_recv,
+):
+    row = lax.axis_index("row")
+    col = lax.axis_index("col")
+    plane, core = col // 2, col % 2
+    half = sigma_ref.shape[1]
+    spans = structure_ref.shape[1]
+    block = factor_ref.shape[0] // spans
+    width = factor_ref.shape[1]
+
+    load_factor = pltpu.make_async_copy(factor_ref, tri, local_sem.at[0])
+    load_factor.start()
+    keep_low = pltpu.make_async_copy(sigma_ref.at[pl.ds(0, half)], held.at[row, col, 0], local_sem.at[1])
+    keep_high = pltpu.make_async_copy(sigma_ref.at[pl.ds(half, half)], held.at[row, col, 1], local_sem.at[2])
+    keep_low.start()
+    keep_high.start()
+
+    sibling = (row, flip(col, 1))
+    beside = {e: (flip(row, e), col) for e in (ALONG_X, ALONG_Y)}
+    line = {s: (row, flip(plane, s) * 2 + core) for s in range(1, planes)}
+    greeted = [sibling, *beside.values(), *line.values()]
+    barrier = pltpu.get_barrier_semaphore()
+    for device in greeted:
+        pl.semaphore_signal(barrier, inc=1, device_id=device, device_id_type=MESH)
+    pl.semaphore_wait(barrier, len(greeted))
+
+    def piece(e, s, which, extra):
+        rr, zz = flip(row, e), flip(plane, s)
+        h = jnp.where(rr > zz, 1 - which, which)
+        return held.at[rr, zz * 2 + which, 1 - h if extra else h]
+
+    def both(e, s, act):
+        act(0)
+
+        @pl.when(flip(row, e) == flip(plane, s))
+        def _():
+            act(1)
+
+    def copy(e, s, extra, device, send, recv, landing, first=False):
+        which = core if landing is None else landing
+        source = piece(e, s, which, extra)
+        target = source
+        if first:
+            h = jnp.where(row > plane, 1 - core, core)
+            h = 1 - h if extra else h
+            source = sigma_ref.at[pl.ds(pl.multiple_of(h * half, half), half)]
+        return pltpu.make_async_remote_copy(
+            src_ref=source, dst_ref=target, send_sem=send.at[extra], recv_sem=recv.at[extra],
+            device_id=device, device_id_type=MESH)
+
+    pending = []
+
+    def post(e, s, device, send, recv, first=False):
+        both(e, s, lambda extra: copy(e, s, extra, device, send, recv, None, first).start())
+        pending.append((e, s, device, send, recv, first))
+
+    def arrive(e, s, device, send, recv, which=None):
+        both(e, s, lambda extra: copy(e, s, extra, device, send, recv, which).wait_recv())
+
+    def to_line(s):
+        post(OWN, 0, line[s], line_send.at[s], line_recv.at[s], True)
+
+    def to_pair(e, s, via, kind, first=False):
+        post(e, s, beside[via], pair_send.at[kind, s], pair_recv.at[kind, s], first)
+
+    def to_core(e, s, first=False):
+        post(e, s, sibling, core_send.at[e, s], core_recv.at[e, s], first)
+
+    def from_pair(e, s):
+        arrive(e, s, beside[ALONG_X], pair_send.at[e, s], pair_recv.at[e, s])
+
+    def spread(s):
+        from_pair(ALONG_X, s)
+        if s % 2 == 0:
+            to_pair(ALONG_X, s, ALONG_Y, ACROSS)
+        to_core(ALONG_X, s)
+        from_pair(ALONG_Y, s)
+        if s % 2 == 1:
+            to_pair(ALONG_Y, s, ALONG_X, ACROSS)
+        to_core(ALONG_Y, s)
+
+    to_pair(OWN, 0, ALONG_X, ALONG_X, True)
+    to_pair(OWN, 0, ALONG_Y, ALONG_Y, True)
+    for s in range(1, planes):
+        to_line(s)
+    to_core(OWN, 0, True)
+
+    for s in range(1, planes):
+        arrive(OWN, s, line[s], line_send.at[s], line_recv.at[s])
+        to_pair(OWN, s, ALONG_X, ALONG_X)
+        to_pair(OWN, s, ALONG_Y, ALONG_Y)
+        to_core(OWN, s)
+        spread(s - 1)
+    spread(planes - 1)
+
+    load_factor.wait()
+    for s in range(planes):
+        from_pair(ACROSS, s)
+        to_core(ACROSS, s)
+    keep_low.wait()
+    keep_high.wait()
+    for e in range(spans):
+        for s in range(planes):
+            arrive(e, s, sibling, core_send.at[e, s], core_recv.at[e, s], 1 - core)
+
+    def put(p, q, a, b, value):
+        gram[p, q, a * half:(a + 1) * half, b * half:(b + 1) * half] = value
+
+    for p in range(spans):
+        for a in range(2):
+            for b in range(2):
+                put(p, p, a, b, held[p, 2 * p + b, a])
+        for q in range(p + 1, spans):
+            for a in range(2):
+                upper = held[p, 2 * q + a, a]
+                put(p, q, a, a, upper)
+                put(q, p, a, a, upper.T)
+                lower = held[q, 2 * p + a, 1 - a]
+                put(q, p, 1 - a, a, lower)
+                put(p, q, a, 1 - a, lower.T)
+
+    tile = block
+    steps = width // tile
+
+    def out_copy(n):
+        cols = pl.ds(pl.multiple_of(n * tile, tile), tile)
+        return pltpu.make_async_copy(result.at[:, cols], out_ref.at[:, cols], out_sem.at[n])
+
+    def step(n, _):
+        cols = pl.ds(pl.multiple_of(n * tile, tile), tile)
+        total = jnp.zeros((1, tile), jnp.float32)
+        for i in range(spans):
+            own = jnp.concatenate([gram[structure_ref[0, i], structure_ref[0, m]] for m in range(spans)], axis=1)
+            product = -jnp.dot(own, tri[:, cols], preferred_element_type=jnp.float32)
+            result[i * block:(i + 1) * block, cols] = product.astype(jnp.bfloat16)
+            total += jnp.sum(tri[i * block:(i + 1) * block, cols].astype(jnp.float32) * product, axis=0, keepdims=True)
+        var_ref[:, cols] = diag_ref[:, cols] - total
+        out_copy(n).start()
+        return 0
+
+    lax.fori_loop(0, steps, step, 0)
+    for n in range(steps):
+        out_copy(n).wait()
+    for e, s, device, send, recv, first in pending:
+        both(e, s, lambda extra: copy(e, s, extra, device, send, recv, None, first).wait_send())
+
+
+def gathered(planes, sigma_anc, structure, factor, diag_term):
+    rows, half = sigma_anc.shape
+    spans = structure.shape[1]
+    depth, width = factor.shape[1:]
+    anywhere = pl.BlockSpec(memory_space=pl.ANY)
+    in_vmem = pl.BlockSpec(memory_space=pltpu.VMEM)
+    dma = pltpu.SemaphoreType.DMA
+    off, variance = pl.pallas_call(
+        functools.partial(kernel, planes),
+        out_shape=(
+            jax.ShapeDtypeStruct((depth, width), jnp.bfloat16),
+            jax.ShapeDtypeStruct((1, width), jnp.float32),
+        ),
+        in_specs=[anywhere, pl.BlockSpec(memory_space=pltpu.SMEM), anywhere, in_vmem],
+        out_specs=(anywhere, in_vmem),
+        scratch_shapes=[
+            pltpu.VMEM((spans, 2 * planes, 2, half, half), jnp.bfloat16),
+            pltpu.VMEM((spans, spans, 2 * half, 2 * half), jnp.bfloat16),
+            pltpu.VMEM((depth, width), jnp.bfloat16),
+            pltpu.VMEM((depth, width), jnp.bfloat16),
+            dma((3,)),
+            dma((spans,)),
+            dma((planes, 2)),
+            dma((planes, 2)),
+            dma((4, planes, 2)),
+            dma((4, planes, 2)),
+            dma((4, planes, 2)),
+            dma((4, planes, 2)),
+        ],
+        compiler_params=pltpu.CompilerParams(
+            collective_id=0, has_side_effects=True, vmem_limit_bytes=48 * 1024 * 1024
+        ),
+        cost_estimate=pl.CostEstimate(
+            flops=2 * depth * depth * width, bytes_accessed=4 * depth * width, transcendentals=0
+        ),
+    )(sigma_anc, structure, factor[0], diag_term)
+    return off[None], variance
+
+
+def selected(sigma_anc, structure, factor, diag_term):
     span_count = structure.shape[1]
     block_rows = factor.shape[1] // span_count
     own_blocks = structure[0]
@@ -24,6 +245,14 @@
 
 
 def solution(mesh):
+    rows, planes = mesh.shape["row"], mesh.shape["col"] // 2
+
+    def body(sigma_anc, structure, factor, diag_term):
+        spans = structure.shape[1]
+        if rows == spans == planes == ACROSS + 1 and sigma_anc.shape[0] == 2 * sigma_anc.shape[1]:
+            return gathered(planes, sigma_anc, structure, factor, diag_term)
+        return selected(sigma_anc, structure, factor, diag_term)
+
     return jax.shard_map(
         body,
         mesh=mesh,

time: 68.4 us -> 32.8 us (0.48); the launches traced: 67.2 us -> 32.5 us
  Pallas kernels: 0 us -> 26.2 us
  blocking collectives: 24.8 us -> 0 us
  waiting for transfers between devices: 24.8 us -> 0 us
  matrix products: 6.06 us -> 0 us
  starting transfers between devices: 3.74 us -> 0 us
  other arithmetic: 2.72 us -> 0 us
  local copies, waits for them, and re-layouts: 4.43 us -> 5.68 us
    pallas_call x0 -> x1, Pallas kernels: none -> 26.2 us  [gathered(): pl.pallas_call(functools.partial(kernel, planes), out_shape=(jax.ShapeDty...]
    all_gather x2 -> x0, blocking collectives: 24.8 us -> none  [the longest x1 17.7 us: body(): panel = lax.all_gather(sigma_anc, 'col', axis=1, tiled=True)]
    all_to_all x1 -> x0, waiting for transfers between devices: 24.8 us -> none  [body(): lax.all_to_all(outgoing, 'row', split_axis=1, concat_axis=1, tiled=True)]
    dot_general x1 -> x0, matrix products: 6.06 us -> none  [body(): jnp.einsum('bim,mw->ibw', picked, triangle, preferred_element_type=jnp.fl...]
    unnamed x9 -> x10, local copies, waits for them, and re-layouts: 1.17 us -> 5.68 us
    all_to_all x1 -> x0, starting transfers between devices: 3.74 us -> none  [body(): lax.all_to_all(outgoing, 'row', split_axis=1, concat_axis=1, tiled=True)]
    gather x3 -> x0, local copies, waits for them, and re-layouts: 2.97 us -> none  [the longest x1 2.01 us: body(): picked = jnp.take(received, own_blocks, axis=1)]
    select_n x3 -> x0, other arithmetic: 1.55 us -> none  [the longest x2 1.54 us: body(): outgoing = jnp.take(blocked, structures, axis=1)]
  transfers between devices with their start and end apart: 1 -> 0, of which waited for: 1 -> 0; matrix products, arithmetic and copies ran while one was open for 0% -> 0% of each run, Pallas kernels for 0% -> 0%
where the time goes in v1:
time: 32.8 us; the launch traced here: 32.5 us
  Pallas kernels  26.2 us (80%)
  local copies, waits for them, and re-layouts  5.68 us (17%)
  between operations  0.65 us (2%)
    pallas_call x1, Pallas kernels, gathered(): pl.pallas_call(functools.partial(kernel, planes), out_shape=(jax.ShapeDty...  26.2 us
    unnamed x10, local copies, waits for them, and re-layouts  5.68 us

profile of v1, /device:TPU:1, one launch (start us, length us, event | category | flops | bytes accessed | tf_op | source)
XLA Modules:
  0.0 32.5 jit_solution(2693997068540469359)
XLA Ops:
  0.6 0.0 copy-start
  0.6 1.6 %copy-done = bf16[1,1024,1024]{2,1,0:T(8,128)(2,1)S(1)} copy-done((bf16[1,1024,1024]{2,1,0:T(8,128)(2,1)S(1)}, bf16[1,1024,1024]{2,1,0:T(8,128)(2,1)}, u32[]{:S(2)}) %copy-start) | copy-done | bytes 2097176
  2.2 0.0 copy-start.1
  2.2 0.8 %copy-done.1 = bf16[256,128]{1,0:T(8,128)(2,1)S(1)} copy-done((bf16[256,128]{1,0:T(8,128)(2,1)S(1)}, bf16[256,128]{1,0:T(8,128)(2,1)}, u32[]{:S(2)}) %copy-start.1) | copy-done | bytes 65560
  3.1 0.0 copy-start.2
  3.1 0.7 %copy-done.2 = f32[1,1024]{1,0:T(1,128)S(1)} copy-done((f32[1,1024]{1,0:T(1,128)S(1)}, f32[1,1024]{1,0:T(1,128)}, u32[]{:S(2)}) %copy-start.2) | copy-done | bytes 4120
  3.8 0.0 copy-start.3
  3.8 0.7 %copy-done.3 = s32[1,4]{1,0:T(1,128)S(1)} copy-done((s32[1,4]{1,0:T(1,128)S(1)}, s32[1,4]{1,0:T(1,128)}, u32[]{:S(2)}) %copy-start.3) | copy-done | bytes 40
  4.4 26.2 %shard_map.59 = (bf16[1024,1024]{1,0:T(8,128)(2,1)S(1)}, f32[1,1024]{1,0:T(1,128)S(1)}) custom-call(bf16[256,128]{1,0:T(8,128)(2,1)S(1)} %copy-done.1, s32[1,4]{1,0:T(1,128)S(1)} %copy-done.3, bf16[1024,1024]{1,0:T(8,128)(2,1)S(1)} %bitcast.3, f32[1,1024]{1,0:T(1,128)S(1)} %copy-done.2), custom_call_target="tpu_custom_call" | custom-call | flops 2147483648 | bytes 4194304 | tf_op jit(solution)/shard_map/pallas_call | solution.py:196
  30.6 1.3 %copy.8 = bf16[1,1024,1024]{2,1,0:T(8,128)(2,1)} copy(bf16[1,1024,1024]{2,1,0:T(8,128)(2,1)S(1)} %bitcast.2) | data formatting | bytes 4194304
  31.9 0.6 %copy.9 = f32[1,1024]{1,0:T(1,128)} copy(f32[1,1024]{1,0:T(1,128)S(1)} %get-tuple-element.9) | data formatting | bytes 8192
Async XLA Ops:
  0.6 1.6 %copy-start = (bf16[1,1024,1024]{2,1,0:T(8,128)(2,1)S(1)}, bf16[1,1024,1024]{2,1,0:T(8,128)(2,1)}, u32[]{:S(2)}) copy-start(bf16[1,1024,1024]{2,1,0:T(8,128)(2,1)} %param.6) | copy-start | bytes 6291460
  2.2 0.8 %copy-start.1 = (bf16[256,128]{1,0:T(8,128)(2,1)S(1)}, bf16[256,128]{1,0:T(8,128)(2,1)}, u32[]{:S(2)}) copy-start(bf16[256,128]{1,0:T(8,128)(2,1)} %sigma_ref.1) | copy-start | bytes 196612
  3.1 0.7 %copy-start.2 = (f32[1,1024]{1,0:T(1,128)S(1)}, f32[1,1024]{1,0:T(1,128)}, u32[]{:S(2)}) copy-start(f32[1,1024]{1,0:T(1,128)} %diag_ref.1) | copy-start | bytes 12292
  3.8 0.7 %copy-start.3 = (s32[1,4]{1,0:T(1,128)S(1)}, s32[1,4]{1,0:T(1,128)}, u32[]{:S(2)}) copy-start(s32[1,4]{1,0:T(1,128)} %structure_ref.1) | copy-start | bytes 52

commit v2 on v1

v2 whole, which is shorter than its diff:
```python
import functools

import jax
import jax.numpy as jnp
from jax import lax
from jax.experimental import pallas as pl
from jax.experimental.pallas import tpu as pltpu
from jax.sharding import PartitionSpec as P

MESH = pl.DeviceIdType.MESH
OWN, ALONG_X, ALONG_Y, ACROSS = range(4)


def flip(value, mask):
    bit = 1
    while bit <= mask:
        if mask & bit:
            value = value + bit - 2 * bit * ((value // bit) % 2)
        bit *= 2
    return value


def kernel(
    planes,
    sigma_ref,
    structure_ref,
    factor_ref,
    diag_ref,
    out_ref,
    var_ref,
    held,
    gram,
    tri,
    result,
    blocks,
    diag,
    local_sem,
    out_sem,
    send_sem,
    extra_sem,
    line_sem,
    pair_sem,
    core_sem,
):
    row = lax.axis_index("row")
    col = lax.axis_index("col")
    plane, core = col // 2, col % 2
    half = sigma_ref.shape[1]
    spans = structure_ref.shape[1]
    block = factor_ref.shape[0] // spans
    width = factor_ref.shape[1]

    def take(h):
        return sigma_ref.at[pl.ds(pl.multiple_of(h * half, half), half)]

    main = take(jnp.where(row > plane, 1 - core, core))
    extra = take(1 - core)
    on_diagonal = row == plane

    keep = pltpu.make_async_copy(main, held.at[0, 0, 0], local_sem.at[0])
    keep_extra = pltpu.make_async_copy(extra, held.at[0, 0, planes], local_sem.at[1])
    load_factor = pltpu.make_async_copy(factor_ref, tri, local_sem.at[2])
    load_blocks = pltpu.make_async_copy(structure_ref, blocks, local_sem.at[3])
    load_diag = pltpu.make_async_copy(diag_ref, diag, local_sem.at[4])
    keep.start()
    pl.when(on_diagonal)(keep_extra.start)

    sibling = (row, col + 1 - 2 * core)
    beside = {e: (flip(row, e), col) for e in (ALONG_X, ALONG_Y)}
    line = {s: (row, flip(plane, s) * 2 + core) for s in range(1, planes)}
    greeted = [*line.values(), *beside.values(), sibling]
    barrier = pltpu.get_barrier_semaphore()
    for device in greeted:
        pl.semaphore_signal(barrier, inc=1, device_id=device, device_id_type=MESH)
    load_factor.start()
    load_blocks.start()
    load_diag.start()
    pl.semaphore_wait(barrier, len(greeted))

    sent = []

    def remote(source, target, recv, device, send=send_sem):
        return pltpu.make_async_remote_copy(
            src_ref=source, dst_ref=target, send_sem=send, recv_sem=recv,
            device_id=device, device_id_type=MESH)

    def to_line(s):
        remote(main, held.at[0, 0, s], line_sem.at[s], line[s]).start()
        sent.append(1)

    def from_line(s):
        remote(held.at[0, 0, s], held.at[0, 0, s], line_sem.at[s], line[1]).wait_recv()

    def extra_to_line(s):
        return remote(extra, held.at[0, 0, planes], line_sem.at[0], line[s], extra_sem.at[s])

    def to_pair(e, via, s, source=None):
        source = held.at[e, 0, s] if source is None else source
        remote(source, held.at[e + via, 0, s], pair_sem.at[e + via, s], beside[via]).start()
        sent.append(1)

    def from_pair(e, s):
        remote(held.at[e, 0, s], held.at[e, 0, s], pair_sem.at[e, s], beside[ALONG_X]).wait_recv()

    parts = ((0, 2), (2, planes + 1))

    def to_core(e, part):
        lo, hi = parts[part]
        remote(held.at[e, 0, lo:hi], held.at[e, 1, lo:hi], core_sem.at[e, part], sibling).start()
        sent.append(hi - lo)

    def from_core(e):
        for part, (lo, hi) in enumerate(parts):
            remote(held.at[e, 1, lo:hi], held.at[e, 1, lo:hi], core_sem.at[e, part], sibling).wait_recv()

    to_pair(OWN, ALONG_X, 0, main)
    to_pair(OWN, ALONG_Y, 0, main)
    for s in range(1, planes):
        to_line(s)

    @pl.when(on_diagonal)
    def _():
        for s in range(1, planes):
            extra_to_line(s).start()

    keep.wait()
    for s in range(1, planes):
        from_line(s)
        to_pair(OWN, ALONG_X, s)
        to_pair(OWN, ALONG_Y, s)
        if s == 1:
            to_core(OWN, 0)
            from_pair(ALONG_X, 0)
            to_pair(ALONG_X, ALONG_Y, 0)
            from_pair(ALONG_Y, 0)

    @pl.when(on_diagonal)
    def _():
        keep_extra.wait()

    @pl.when(jnp.logical_not(on_diagonal))
    def _():
        extra_to_line(1).wait_recv()

    to_pair(OWN, ALONG_X, planes)
    to_pair(OWN, ALONG_Y, planes)
    to_core(OWN, 1)
    for s in range(1, planes + 1):
        from_pair(ALONG_X, s)
        if s == planes:
            to_pair(ALONG_X, ALONG_Y, s)
        from_pair(ALONG_Y, s)
        if s < planes:
            to_pair(ALONG_Y, ALONG_X, s)
        if s == 1:
            to_core(ALONG_X, 0)
            to_core(ALONG_Y, 0)
    to_core(ALONG_X, 1)
    to_core(ALONG_Y, 1)

    differ, bit = 0, 1
    while bit < planes:
        one, two = (row // bit) % 2, (plane // bit) % 2
        differ = differ + bit * (one + two - 2 * one * two)
        bit *= 2
    at_row = [flip(row, e) for e in range(spans)]
    at_plane = [flip(differ, e) for e in range(spans)]

    def put(p, q, a, b, value):
        gram[p, q, a * half:(a + 1) * half, b * half:(b + 1) * half] = value

    def other(which):
        return which + core - 2 * which * core

    def diagonal(e):
        p = at_row[e]
        for which in range(2):
            put(p, p, which, which, held[e, other(which), at_plane[e]])
            put(p, p, 1 - which, which, held[e, other(which), planes])

    def off_diagonal(e, f):
        up = at_row[e] < at_row[f]
        lo, hi = jnp.where(up, e, f), jnp.where(up, f, e)
        p, q = jnp.where(up, at_row[e], at_row[f]), jnp.where(up, at_row[f], at_row[e])
        p_plane, q_plane = jnp.where(up, at_plane[e], at_plane[f]), jnp.where(up, at_plane[f], at_plane[e])
        for which in range(2):
            upper = held[lo, other(which), q_plane]
            put(p, q, which, which, upper)
            put(q, p, which, which, upper.T)
            lower = held[hi, other(which), p_plane]
            put(q, p, 1 - which, which, lower)
            put(p, q, which, 1 - which, lower.T)

    from_core(OWN)
    diagonal(OWN)
    from_core(ALONG_X)
    diagonal(ALONG_X)
    off_diagonal(OWN, ALONG_X)
    from_pair(ACROSS, 0)
    from_pair(ACROSS, 1)
    to_core(ACROSS, 0)
    from_core(ALONG_Y)
    diagonal(ALONG_Y)
    off_diagonal(OWN, ALONG_Y)
    off_diagonal(ALONG_X, ALONG_Y)
    for s in range(2, planes + 1):
        from_pair(ACROSS, s)
    to_core(ACROSS, 1)
    load_factor.wait()
    load_blocks.wait()
    load_diag.wait()
    from_core(ACROSS)
    diagonal(ACROSS)
    for e in (OWN, ALONG_X, ALONG_Y):
        off_diagonal(e, ACROSS)

    tile = block
    steps = width // tile

    def out_copy(n):
        cols = pl.ds(pl.multiple_of(n * tile, tile), tile)
        return pltpu.make_async_copy(result.at[:, cols], out_ref.at[:, cols], out_sem.at[n])

    def step(n, _):
        cols = pl.ds(pl.multiple_of(n * tile, tile), tile)
        total = jnp.zeros((1, tile), jnp.float32)
        for i in range(spans):
            own = jnp.concatenate([gram[blocks[0, i], blocks[0, m]] for m in range(spans)], axis=1)
            product = -jnp.dot(own, tri[:, cols], preferred_element_type=jnp.float32)
            result[i * block:(i + 1) * block, cols] = product.astype(jnp.bfloat16)
            total += jnp.sum(tri[i * block:(i + 1) * block, cols].astype(jnp.float32) * product, axis=0, keepdims=True)
        var_ref[:, cols] = diag[:, cols] - total
        out_copy(n).start()
        return 0

    lax.fori_loop(0, steps, step, 0)

    same_bytes = tri.at[0:sum(sent) * half * half // width]
    pltpu.make_async_copy(same_bytes, same_bytes, send_sem).wait()

    @pl.when(on_diagonal)
    def _():
        for s in range(1, planes):
            extra_to_line(s).wait_send()

    for n in range(steps):
        out_copy(n).wait()


def gathered(planes, sigma_anc, structure, factor, diag_term):
    rows, half = sigma_anc.shape
    spans = structure.shape[1]
    depth, width = factor.shape[1:]
    anywhere = pl.BlockSpec(memory_space=pl.ANY)
    in_vmem = pl.BlockSpec(memory_space=pltpu.VMEM)
    dma = pltpu.SemaphoreType.DMA
    off, variance = pl.pallas_call(
        functools.partial(kernel, planes),
        out_shape=(
            jax.ShapeDtypeStruct((depth, width), jnp.bfloat16),
            jax.ShapeDtypeStruct((1, width), jnp.float32),
        ),
        in_specs=[anywhere] * 4,
        out_specs=(anywhere, in_vmem),
        scratch_shapes=[
            pltpu.VMEM((spans, 2, planes + 1, half, half), jnp.bfloat16),
            pltpu.VMEM((spans, spans, 2 * half, 2 * half), jnp.bfloat16),
            pltpu.VMEM((depth, width), jnp.bfloat16),
            pltpu.VMEM((depth, width), jnp.bfloat16),
            pltpu.SMEM((1, spans), jnp.int32),
            pltpu.VMEM((1, width), jnp.float32),
            dma((5,)),
            dma((spans,)),
            dma(()),
            dma((planes,)),
            dma((planes,)),
            dma((spans, planes + 1)),
            dma((spans, 2)),
        ],
        compiler_params=pltpu.CompilerParams(
            collective_id=0, has_side_effects=True, vmem_limit_bytes=60 * 1024 * 1024
        ),
        cost_estimate=pl.CostEstimate(
            flops=2 * depth * depth * width, bytes_accessed=4 * depth * width, transcendentals=0
        ),
    )(sigma_anc, structure, factor[0], diag_term)
    return off[None], variance


def selected(sigma_anc, structure, factor, diag_term):
    span_count = structure.shape[1]
    block_rows = factor.shape[1] // span_count
    own_blocks = structure[0]
    triangle = factor[0]
    panel = lax.all_gather(sigma_anc, "col", axis=1, tiled=True)
    structures = lax.all_gather(structure, "row", axis=0, tiled=True)
    block_total = panel.shape[1] // block_rows
    blocked = panel.reshape(block_rows, block_total, block_rows)
    outgoing = jnp.take(blocked, structures, axis=1)
    outgoing = outgoing.reshape(block_rows, structures.shape[0], span_count * block_rows)
    received = lax.all_to_all(outgoing, "row", split_axis=1, concat_axis=1, tiled=True)
    picked = jnp.take(received, own_blocks, axis=1)
    product = jnp.einsum("bim,mw->ibw", picked, triangle, preferred_element_type=jnp.float32)
    off_block = -product.reshape(span_count * block_rows, triangle.shape[1])
    variance = diag_term[0] - jnp.sum(triangle.astype(jnp.float32) * off_block, axis=0)
    return (off_block.astype(jnp.bfloat16)[None], variance[None])


def solution(mesh):
    rows, planes = mesh.shape["row"], mesh.shape["col"] // 2

    def body(sigma_anc, structure, factor, diag_term):
        spans = structure.shape[1]
        if rows == spans == planes == ACROSS + 1 and sigma_anc.shape[0] == 2 * sigma_anc.shape[1]:
            return gathered(planes, sigma_anc, structure, factor, diag_term)
        return selected(sigma_anc, structure, factor, diag_term)

    return jax.shard_map(
        body,
        mesh=mesh,
        in_specs=(
            P("row", "col"),
            P(("row", "col"), None),
            P(("row", "col"), None, None),
            P(("row", "col"), None),
        ),
        out_specs=(P(("row", "col"), None, None), P(("row", "col"), None)),
        check_vma=False,
    )
```

time: 32.8 us -> 28.4 us (0.87)
  Pallas kernels: 26.2 us -> 23.9 us
  local copies, waits for them, and re-layouts: 5.68 us -> 3.68 us
    pallas_call x1, Pallas kernels: 26.2 us -> 23.9 us  [gathered(): pl.pallas_call(functools.partial(kernel, planes), out_shape=(jax.ShapeDty...]
    unnamed x10 -> x4, local copies, waits for them, and re-layouts: 5.68 us -> 3.68 us
where the time goes in v2:
time: 28.4 us; the launch traced here: 28.2 us
  Pallas kernels  23.9 us (84%)
  local copies, waits for them, and re-layouts  3.68 us (13%)
  between operations  0.65 us (2%)
    pallas_call x1, Pallas kernels, gathered(): pl.pallas_call(functools.partial(kernel, planes), out_shape=(jax.ShapeDty...  23.9 us
    unnamed x4, local copies, waits for them, and re-layouts  3.68 us

profile of v2, /device:TPU:1, one launch (start us, length us, event | category | flops | bytes accessed | tf_op | source)
XLA Modules:
  0.0 28.2 jit_solution(17184368899103641595)
XLA Ops:
  0.6 23.9 %shard_map.59 = (bf16[1024,1024]{1,0:T(8,128)(2,1)}, f32[1,1024]{1,0:T(1,128)}) custom-call(bf16[256,128]{1,0:T(8,128)(2,1)} %sigma_ref.1, s32[1,4]{1,0:T(1,128)} %structure_ref.1, bf16[1024,1024]{1,0:T(8,128)(2,1)} %bitcast.3, f32[1,1024]{1,0:T(1,128)} %diag_ref.1), custom_call_target="tpu_custom_call" | custom-call | flops 2147483648 | bytes 4194304 | tf_op jit(solution)/shard_map/pallas_call | solution.py:257
  24.5 0.0 copy-start
  24.5 3.1 %copy.8 = bf16[1,1024,1024]{2,1,0:T(8,128)(2,1)} copy(bf16[1,1024,1024]{2,1,0:T(8,128)(2,1)} %bitcast.2) | data formatting | bytes 4194304
  27.6 0.0 copy-done
  27.6 0.6 %copy.9 = f32[1,1024]{1,0:T(1,128)} copy(f32[1,1024]{1,0:T(1,128)S(1)} %copy-done) | data formatting | bytes 8192
Async XLA Ops:
  24.5 3.1 %copy-start = (f32[1,1024]{1,0:T(1,128)S(1)}, f32[1,1024]{1,0:T(1,128)}, u32[]{:S(2)}) copy-start(f32[1,1024]{1,0:T(1,128)} %get-tuple-element.9) | copy-start | bytes 12292

commit v3 on v2

--- a/solution.py
+++ b/solution.py
@@ -23,19 +23,10 @@
 def kernel(
     planes,
     sigma_ref,
-    structure_ref,
-    factor_ref,
-    diag_ref,
-    out_ref,
-    var_ref,
+    gram,
     held,
-    gram,
-    tri,
-    result,
-    blocks,
-    diag,
+    total,
     local_sem,
-    out_sem,
     send_sem,
     extra_sem,
     line_sem,
@@ -46,9 +37,7 @@
     col = lax.axis_index("col")
     plane, core = col // 2, col % 2
     half = sigma_ref.shape[1]
-    spans = structure_ref.shape[1]
-    block = factor_ref.shape[0] // spans
-    width = factor_ref.shape[1]
+    spans = gram.shape[0]
 
     def take(h):
         return sigma_ref.at[pl.ds(pl.multiple_of(h * half, half), half)]
@@ -59,9 +48,6 @@
 
     keep = pltpu.make_async_copy(main, held.at[0, 0, 0], local_sem.at[0])
     keep_extra = pltpu.make_async_copy(extra, held.at[0, 0, planes], local_sem.at[1])
-    load_factor = pltpu.make_async_copy(factor_ref, tri, local_sem.at[2])
-    load_blocks = pltpu.make_async_copy(structure_ref, blocks, local_sem.at[3])
-    load_diag = pltpu.make_async_copy(diag_ref, diag, local_sem.at[4])
     keep.start()
     pl.when(on_diagonal)(keep_extra.start)
 
@@ -72,9 +58,6 @@
     barrier = pltpu.get_barrier_semaphore()
     for device in greeted:
         pl.semaphore_signal(barrier, inc=1, device_id=device, device_id_type=MESH)
-    load_factor.start()
-    load_blocks.start()
-    load_diag.start()
     pl.semaphore_wait(barrier, len(greeted))
 
     sent = []
@@ -206,14 +189,24 @@
     for s in range(2, planes + 1):
         from_pair(ACROSS, s)
     to_core(ACROSS, 1)
-    load_factor.wait()
-    load_blocks.wait()
-    load_diag.wait()
     from_core(ACROSS)
     diagonal(ACROSS)
     for e in (OWN, ALONG_X, ALONG_Y):
         off_diagonal(e, ACROSS)
 
+    same_bytes = total.at[0:sum(sent)]
+    pltpu.make_async_copy(same_bytes, same_bytes, send_sem).wait()
+
+    @pl.when(on_diagonal)
+    def _():
+        for s in range(1, planes):
+            extra_to_line(s).wait_send()
+
+
+def multiply(structure_ref, gram, tri, diag_ref, out_ref, var_ref, result, out_sem):
+    spans = gram.shape[0]
+    block = gram.shape[2]
+    width = tri.shape[1]
     tile = block
     steps = width // tile
 
@@ -225,24 +218,15 @@
         cols = pl.ds(pl.multiple_of(n * tile, tile), tile)
         total = jnp.zeros((1, tile), jnp.float32)
         for i in range(spans):
-            own = jnp.concatenate([gram[blocks[0, i], blocks[0, m]] for m in range(spans)], axis=1)
+            own = jnp.concatenate([gram[structure_ref[0, i], structure_ref[0, m]] for m in range(spans)], axis=1)
             product = -jnp.dot(own, tri[:, cols], preferred_element_type=jnp.float32)
             result[i * block:(i + 1) * block, cols] = product.astype(jnp.bfloat16)
             total += jnp.sum(tri[i * block:(i + 1) * block, cols].astype(jnp.float32) * product, axis=0, keepdims=True)
-        var_ref[:, cols] = diag[:, cols] - total
+        var_ref[:, cols] = diag_ref[:, cols] - total
         out_copy(n).start()
         return 0
 
     lax.fori_loop(0, steps, step, 0)
-
-    same_bytes = tri.at[0:sum(sent) * half * half // width]
-    pltpu.make_async_copy(same_bytes, same_bytes, send_sem).wait()
-
-    @pl.when(on_diagonal)
-    def _():
-        for s in range(1, planes):
-            extra_to_line(s).wait_send()
-
     for n in range(steps):
         out_copy(n).wait()
 
@@ -252,25 +236,20 @@
     spans = structure.shape[1]
     depth, width = factor.shape[1:]
     anywhere = pl.BlockSpec(memory_space=pl.ANY)
+    in_hbm = pl.BlockSpec(memory_space=pltpu.HBM)
     in_vmem = pl.BlockSpec(memory_space=pltpu.VMEM)
+    in_smem = pl.BlockSpec(memory_space=pltpu.SMEM)
     dma = pltpu.SemaphoreType.DMA
-    off, variance = pl.pallas_call(
+    pieces = spans * 2 * (planes + 1)
+    gram = pl.pallas_call(
         functools.partial(kernel, planes),
-        out_shape=(
-            jax.ShapeDtypeStruct((depth, width), jnp.bfloat16),
-            jax.ShapeDtypeStruct((1, width), jnp.float32),
-        ),
-        in_specs=[anywhere] * 4,
-        out_specs=(anywhere, in_vmem),
+        out_shape=jax.ShapeDtypeStruct((spans, spans, 2 * half, 2 * half), jnp.bfloat16),
+        in_specs=[in_hbm],
+        out_specs=in_vmem,
         scratch_shapes=[
             pltpu.VMEM((spans, 2, planes + 1, half, half), jnp.bfloat16),
-            pltpu.VMEM((spans, spans, 2 * half, 2 * half), jnp.bfloat16),
-            pltpu.VMEM((depth, width), jnp.bfloat16),
-            pltpu.VMEM((depth, width), jnp.bfloat16),
-            pltpu.SMEM((1, spans), jnp.int32),
-            pltpu.VMEM((1, width), jnp.float32),
-            dma((5,)),
-            dma((spans,)),
+            pltpu.VMEM((pieces, half, half), jnp.bfloat16),
+            dma((2,)),
             dma(()),
             dma((planes,)),
             dma((planes,)),
@@ -278,12 +257,24 @@
             dma((spans, 2)),
         ],
         compiler_params=pltpu.CompilerParams(
-            collective_id=0, has_side_effects=True, vmem_limit_bytes=60 * 1024 * 1024
+            collective_id=0, has_side_effects=True, vmem_limit_bytes=16 * 1024 * 1024
         ),
+        cost_estimate=pl.CostEstimate(flops=0, bytes_accessed=16 * depth * depth, transcendentals=0),
+    )(sigma_anc)
+    off, variance = pl.pallas_call(
+        multiply,
+        out_shape=(
+            jax.ShapeDtypeStruct((depth, width), jnp.bfloat16),
+            jax.ShapeDtypeStruct((1, width), jnp.float32),
+        ),
+        in_specs=[in_smem, in_vmem, in_vmem, in_vmem],
+        out_specs=(anywhere, in_vmem),
+        scratch_shapes=[pltpu.VMEM((depth, width), jnp.bfloat16), dma((spans,))],
+        compiler_params=pltpu.CompilerParams(vmem_limit_bytes=24 * 1024 * 1024),
         cost_estimate=pl.CostEstimate(
             flops=2 * depth * depth * width, bytes_accessed=4 * depth * width, transcendentals=0
         ),
-    )(sigma_anc, structure, factor[0], diag_term)
+    )(structure, gram, factor[0], diag_term)
     return off[None], variance
 
 

time: 28.4 us -> 25.9 us (0.912)
  local copies, waits for them, and re-layouts: 3.68 us -> 0.85 us
  Pallas kernels: 23.9 us -> 24.2 us
    unnamed x4 -> x8, local copies, waits for them, and re-layouts: 3.68 us -> 0.85 us
    pallas_call x1 -> x2, Pallas kernels: 23.9 us -> 24.2 us  [the longest x1 19.2 us: gathered(): pl.pallas_call(functools.partial(kernel, planes), out_shape=jax.ShapeDtyp...]
where the time goes in v3:
time: 25.9 us; the launch traced here: 25.7 us
  Pallas kernels  24.2 us (93%)
  local copies, waits for them, and re-layouts  0.85 us (3%)
  between operations  0.68 us (3%)
    pallas_call x1, Pallas kernels, gathered(): pl.pallas_call(functools.partial(kernel, planes), out_shape=jax.ShapeDtyp...  19.2 us
    pallas_call x1, Pallas kernels, gathered(): pl.pallas_call(multiply, out_shape=(jax.ShapeDtypeStruct((depth, width),...  4.96 us
    unnamed x8, local copies, waits for them, and re-layouts  0.85 us

profile of v3, /device:TPU:1, one launch (start us, length us, event | category | flops | bytes accessed | tf_op | source)
XLA Modules:
  0.0 25.7 jit_solution(4012595528611755853)
XLA Ops:
  0.6 0.0 copy-start.3
  0.6 0.0 copy-start
  0.7 0.8 %copy-done = bf16[256,128]{1,0:T(8,128)(2,1)S(1)} copy-done((bf16[256,128]{1,0:T(8,128)(2,1)S(1)}, bf16[256,128]{1,0:T(8,128)(2,1)}, u32[]{:S(2)}) %copy-start) | copy-done | bytes 65560
  1.5 0.0 copy-start.1
  1.5 0.0 copy-start.2
  1.5 19.2 %shard_map.59.gram = bf16[4,4,256,256]{3,2,1,0:T(8,128)(2,1)S(1)} custom-call(bf16[256,128]{1,0:T(8,128)(2,1)S(1)} %copy-done), custom_call_target="tpu_custom_call" | custom-call | bytes 16777216 | tf_op jit(solution)/shard_map/pallas_call | solution.py:244
  20.7 0.0 copy-done.3
  20.7 0.0 copy-done.1
  20.7 0.0 copy-done.2
  20.8 5.0 %shard_map.60 = (bf16[1024,1024]{1,0:T(8,128)(2,1)}, f32[1,1024]{1,0:T(1,128)}) custom-call(s32[1,4]{1,0:T(1,128)S(1)} %copy-done.3, bf16[4,4,256,256]{3,2,1,0:T(8,128)(2,1)S(1)} %shard_map.59.gram, bf16[1024,1024]{1,0:T(8,128)(2,1)S(1)} %bitcast.2, f32[1,1024]{1,0:T(1,128)S(1)} %copy-done.2), custom_call_target="tpu_custom_call" | custom-call | flops 2147483648 | bytes 4194304 | tf_op jit(solution)/shard_map/pallas_call | solution.py:264
Async XLA Ops:
  0.6 20.1 %copy-start.3 = (s32[1,4]{1,0:T(1,128)S(1)}, s32[1,4]{1,0:T(1,128)}, u32[]{:S(2)}) copy-start(s32[1,4]{1,0:T(1,128)} %structure_ref.1) | copy-start | bytes 52
  0.6 0.8 %copy-start = (bf16[256,128]{1,0:T(8,128)(2,1)S(1)}, bf16[256,128]{1,0:T(8,128)(2,1)}, u32[]{:S(2)}) copy-start(bf16[256,128]{1,0:T(8,128)(2,1)} %sigma_ref.1) | copy-start | bytes 196612
  1.5 19.2 %copy-start.1 = (bf16[1,1024,1024]{2,1,0:T(8,128)(2,1)S(1)}, bf16[1,1024,1024]{2,1,0:T(8,128)(2,1)}, u32[]{:S(2)}) copy-start(bf16[1,1024,1024]{2,1,0:T(8,128)(2,1)} %param.6) | copy-start | bytes 6291460
  1.5 19.3 %copy-start.2 = (f32[1,1024]{1,0:T(1,128)S(1)}, f32[1,1024]{1,0:T(1,128)}, u32[]{:S(2)}) copy-start(f32[1,1024]{1,0:T(1,128)} %diag_ref.1) | copy-start | bytes 12292

commit v4 on v3

--- a/solution.py
+++ b/solution.py
@@ -203,7 +203,7 @@
             extra_to_line(s).wait_send()
 
 
-def multiply(structure_ref, gram, tri, diag_ref, out_ref, var_ref, result, out_sem):
+def multiply(structure_ref, gram, tri, diag_ref, out_ref, var_ref, own, result, out_sem):
     spans = gram.shape[0]
     block = gram.shape[2]
     width = tri.shape[1]
@@ -214,14 +214,15 @@
         cols = pl.ds(pl.multiple_of(n * tile, tile), tile)
         return pltpu.make_async_copy(result.at[:, cols], out_ref.at[:, cols], out_sem.at[n])
 
+    for i in range(spans):
+        for m in range(spans):
+            own[i * block:(i + 1) * block, m * block:(m + 1) * block] = gram[structure_ref[0, i], structure_ref[0, m]]
+
     def step(n, _):
         cols = pl.ds(pl.multiple_of(n * tile, tile), tile)
-        total = jnp.zeros((1, tile), jnp.float32)
-        for i in range(spans):
-            own = jnp.concatenate([gram[structure_ref[0, i], structure_ref[0, m]] for m in range(spans)], axis=1)
-            product = -jnp.dot(own, tri[:, cols], preferred_element_type=jnp.float32)
-            result[i * block:(i + 1) * block, cols] = product.astype(jnp.bfloat16)
-            total += jnp.sum(tri[i * block:(i + 1) * block, cols].astype(jnp.float32) * product, axis=0, keepdims=True)
+        product = -jnp.dot(own[...], tri[:, cols], preferred_element_type=jnp.float32)
+        result[:, cols] = product.astype(jnp.bfloat16)
+        total = jnp.sum(tri[:, cols].astype(jnp.float32) * product, axis=0, keepdims=True)
         var_ref[:, cols] = diag_ref[:, cols] - total
         out_copy(n).start()
         return 0
@@ -260,7 +261,7 @@
             collective_id=0, has_side_effects=True, vmem_limit_bytes=16 * 1024 * 1024
         ),
         cost_estimate=pl.CostEstimate(flops=0, bytes_accessed=16 * depth * depth, transcendentals=0),
-    )(sigma_anc)
+    )(pltpu.with_memory_space_constraint(sigma_anc, pltpu.HBM))
     off, variance = pl.pallas_call(
         multiply,
         out_shape=(
@@ -269,7 +270,11 @@
         ),
         in_specs=[in_smem, in_vmem, in_vmem, in_vmem],
         out_specs=(anywhere, in_vmem),
-        scratch_shapes=[pltpu.VMEM((depth, width), jnp.bfloat16), dma((spans,))],
+        scratch_shapes=[
+            pltpu.VMEM((depth, depth), jnp.bfloat16),
+            pltpu.VMEM((depth, width), jnp.bfloat16),
+            dma((spans,)),
+        ],
         compiler_params=pltpu.CompilerParams(vmem_limit_bytes=24 * 1024 * 1024),
         cost_estimate=pl.CostEstimate(
             flops=2 * depth * depth * width, bytes_accessed=4 * depth * width, transcendentals=0

time: 25.9 us -> 25.4 us (0.981)
  local copies, waits for them, and re-layouts: 0.85 us -> 0.01 us
  Pallas kernels: 24.2 us -> 24.6 us
    unnamed x8 -> x6, local copies, waits for them, and re-layouts: 0.85 us -> 0.01 us
where the time goes in v4:
time: 25.4 us; the launch traced here: 25.3 us
  Pallas kernels  24.6 us (97%)
  between operations  0.69 us (3%)
    pallas_call x1, Pallas kernels, gathered(): pl.pallas_call(functools.partial(kernel, planes), out_shape=jax.ShapeDtyp...  19.4 us
    pallas_call x1, Pallas kernels, gathered(): pl.pallas_call(multiply, out_shape=(jax.ShapeDtypeStruct((depth, width),...  5.16 us

profile of v4, /device:TPU:1, one launch (start us, length us, event | category | flops | bytes accessed | tf_op | source)
XLA Modules:
  0.0 25.3 jit_solution(7485737724675273262)
XLA Ops:
  0.6 0.0 copy-start.1
  0.6 0.0 copy-start
  0.7 0.0 copy-start.2
  0.7 19.4 %shard_map.59.gram = bf16[4,4,256,256]{3,2,1,0:T(8,128)(2,1)S(1)} custom-call(bf16[256,128]{1,0:T(8,128)(2,1)} %sigma_ref.1), custom_call_target="tpu_custom_call" | custom-call | bytes 16777216 | tf_op jit(solution)/shard_map/pallas_call | solution.py:245
  20.1 0.0 copy-done.1
  20.1 0.0 copy-done
  20.1 0.0 copy-done.2
  20.1 5.2 %shard_map.60 = (bf16[1024,1024]{1,0:T(8,128)(2,1)}, f32[1,1024]{1,0:T(1,128)}) custom-call(s32[1,4]{1,0:T(1,128)S(1)} %copy-done.2, bf16[4,4,256,256]{3,2,1,0:T(8,128)(2,1)S(1)} %shard_map.59.gram, bf16[1024,1024]{1,0:T(8,128)(2,1)S(1)} %bitcast.2, f32[1,1024]{1,0:T(1,128)S(1)} %copy-done.1), custom_call_target="tpu_custom_call" | custom-call | flops 2147483648 | bytes 4194304 | tf_op jit(solution)/shard_map/pallas_call | solution.py:265
Async XLA Ops:
  0.6 19.5 %copy-start.1 = (f32[1,1024]{1,0:T(1,128)S(1)}, f32[1,1024]{1,0:T(1,128)}, u32[]{:S(2)}) copy-start(f32[1,1024]{1,0:T(1,128)} %diag_ref.1) | copy-start | bytes 12292
  0.6 19.5 %copy-start = (bf16[1,1024,1024]{2,1,0:T(8,128)(2,1)S(1)}, bf16[1,1024,1024]{2,1,0:T(8,128)(2,1)}, u32[]{:S(2)}) copy-start(bf16[1,1024,1024]{2,1,0:T(8,128)(2,1)} %param.6) | copy-start | bytes 6291460
  0.7 19.5 %copy-start.2 = (s32[1,4]{1,0:T(1,128)S(1)}, s32[1,4]{1,0:T(1,128)}, u32[]{:S(2)}) copy-start(s32[1,4]{1,0:T(1,128)} %structure_ref.1) | copy-start | bytes 52

commit v5 on v3

--- a/solution.py
+++ b/solution.py
@@ -203,32 +203,30 @@
             extra_to_line(s).wait_send()
 
 
-def multiply(structure_ref, gram, tri, diag_ref, out_ref, var_ref, result, out_sem):
+def multiply(structure_ref, gram, tri, diag_ref, out_ref, var_ref, result, var, out_sem, var_sem):
     spans = gram.shape[0]
     block = gram.shape[2]
     width = tri.shape[1]
     tile = block
-    steps = width // tile
-
-    def out_copy(n):
-        cols = pl.ds(pl.multiple_of(n * tile, tile), tile)
-        return pltpu.make_async_copy(result.at[:, cols], out_ref.at[:, cols], out_sem.at[n])
-
-    def step(n, _):
-        cols = pl.ds(pl.multiple_of(n * tile, tile), tile)
+    copies = []
+
+    def send(source, target, sem):
+        copies.append(pltpu.make_async_copy(source, target, sem))
+        copies[-1].start()
+
+    for n in range(width // tile):
+        cols = slice(n * tile, (n + 1) * tile)
         total = jnp.zeros((1, tile), jnp.float32)
         for i in range(spans):
             own = jnp.concatenate([gram[structure_ref[0, i], structure_ref[0, m]] for m in range(spans)], axis=1)
             product = -jnp.dot(own, tri[:, cols], preferred_element_type=jnp.float32)
             result[i * block:(i + 1) * block, cols] = product.astype(jnp.bfloat16)
             total += jnp.sum(tri[i * block:(i + 1) * block, cols].astype(jnp.float32) * product, axis=0, keepdims=True)
-        var_ref[:, cols] = diag_ref[:, cols] - total
-        out_copy(n).start()
-        return 0
-
-    lax.fori_loop(0, steps, step, 0)
-    for n in range(steps):
-        out_copy(n).wait()
+        var[:, cols] = diag_ref[:, cols] - total
+        send(result.at[:, cols], out_ref.at[:, cols], out_sem.at[n])
+    send(var, var_ref, var_sem)
+    for copy in copies:
+        copy.wait()
 
 
 def gathered(planes, sigma_anc, structure, factor, diag_term):
@@ -260,7 +258,7 @@
             collective_id=0, has_side_effects=True, vmem_limit_bytes=16 * 1024 * 1024
         ),
         cost_estimate=pl.CostEstimate(flops=0, bytes_accessed=16 * depth * depth, transcendentals=0),
-    )(sigma_anc)
+    )(pltpu.with_memory_space_constraint(sigma_anc, pltpu.HBM))
     off, variance = pl.pallas_call(
         multiply,
         out_shape=(
@@ -268,8 +266,13 @@
             jax.ShapeDtypeStruct((1, width), jnp.float32),
         ),
         in_specs=[in_smem, in_vmem, in_vmem, in_vmem],
-        out_specs=(anywhere, in_vmem),
-        scratch_shapes=[pltpu.VMEM((depth, width), jnp.bfloat16), dma((spans,))],
+        out_specs=(anywhere, anywhere),
+        scratch_shapes=[
+            pltpu.VMEM((depth, width), jnp.bfloat16),
+            pltpu.VMEM((1, width), jnp.float32),
+            dma((width // (depth // spans),)),
+            dma(()),
+        ],
         compiler_params=pltpu.CompilerParams(vmem_limit_bytes=24 * 1024 * 1024),
         cost_estimate=pl.CostEstimate(
             flops=2 * depth * depth * width, bytes_accessed=4 * depth * width, transcendentals=0

time: 25.9 us -> 24.1 us (0.931)
  Pallas kernels: 24.2 us -> 23.3 us
  local copies, waits for them, and re-layouts: 0.85 us -> 0.01 us
    pallas_call x1, Pallas kernels: 4.96 us -> 3.86 us  [gathered(): pl.pallas_call(multiply, out_shape=(jax.ShapeDtypeStruct((depth, width),...]
    unnamed x8 -> x6, local copies, waits for them, and re-layouts: 0.85 us -> 0.01 us
where the time goes in v5:
time: 24.1 us; the launch traced here: 24 us
  Pallas kernels  23.3 us (97%)
  between operations  0.69 us (3%)
    pallas_call x1, Pallas kernels, gathered(): pl.pallas_call(functools.partial(kernel, planes), out_shape=jax.ShapeDtyp...  19.4 us
    pallas_call x1, Pallas kernels, gathered(): pl.pallas_call(multiply, out_shape=(jax.ShapeDtypeStruct((depth, width),...  3.86 us

profile of v5, /device:TPU:1, one launch (start us, length us, event | category | flops | bytes accessed | tf_op | source)
XLA Modules:
  0.0 24.0 jit_solution(6425238492334815323)
XLA Ops:
  0.6 0.0 copy-start.1
  0.6 0.0 copy-start
  0.7 0.0 copy-start.2
  0.7 19.4 %shard_map.59.gram = bf16[4,4,256,256]{3,2,1,0:T(8,128)(2,1)S(1)} custom-call(bf16[256,128]{1,0:T(8,128)(2,1)} %sigma_ref.1), custom_call_target="tpu_custom_call" | custom-call | bytes 16777216 | tf_op jit(solution)/shard_map/pallas_call | solution.py:242
  20.1 0.0 copy-done.1
  20.1 0.0 copy-done
  20.1 0.0 copy-done.2
  20.1 3.9 %shard_map.60 = (bf16[1024,1024]{1,0:T(8,128)(2,1)}, f32[1,1024]{1,0:T(1,128)}) custom-call(s32[1,4]{1,0:T(1,128)S(1)} %copy-done.2, bf16[4,4,256,256]{3,2,1,0:T(8,128)(2,1)S(1)} %shard_map.59.gram, bf16[1024,1024]{1,0:T(8,128)(2,1)S(1)} %bitcast.2, f32[1,1024]{1,0:T(1,128)S(1)} %copy-done.1), custom_call_target="tpu_custom_call" | custom-call | flops 2147483648 | bytes 4194304 | tf_op jit(solution)/shard_map/pallas_call | solution.py:262
Async XLA Ops:
  0.6 19.5 %copy-start.1 = (f32[1,1024]{1,0:T(1,128)S(1)}, f32[1,1024]{1,0:T(1,128)}, u32[]{:S(2)}) copy-start(f32[1,1024]{1,0:T(1,128)} %diag_ref.1) | copy-start | bytes 12292
  0.6 19.5 %copy-start = (bf16[1,1024,1024]{2,1,0:T(8,128)(2,1)S(1)}, bf16[1,1024,1024]{2,1,0:T(8,128)(2,1)}, u32[]{:S(2)}) copy-start(bf16[1,1024,1024]{2,1,0:T(8,128)(2,1)} %param.6) | copy-start | bytes 6291460
  0.7 19.5 %copy-start.2 = (s32[1,4]{1,0:T(1,128)S(1)}, s32[1,4]{1,0:T(1,128)}, u32[]{:S(2)}) copy-start(s32[1,4]{1,0:T(1,128)} %structure_ref.1) | copy-start | bytes 52

commit v6 on v5

--- a/solution.py
+++ b/solution.py
@@ -182,13 +182,13 @@
     from_pair(ACROSS, 0)
     from_pair(ACROSS, 1)
     to_core(ACROSS, 0)
+    for s in range(2, planes + 1):
+        from_pair(ACROSS, s)
+    to_core(ACROSS, 1)
     from_core(ALONG_Y)
     diagonal(ALONG_Y)
     off_diagonal(OWN, ALONG_Y)
     off_diagonal(ALONG_X, ALONG_Y)
-    for s in range(2, planes + 1):
-        from_pair(ACROSS, s)
-    to_core(ACROSS, 1)
     from_core(ACROSS)
     diagonal(ACROSS)
     for e in (OWN, ALONG_X, ALONG_Y):

time: 24.1 us -> 24.1 us (level)
  no operation moved by 1% of the time
where the time goes in v6:
time: 24.1 us; the launch traced here: 24 us
  Pallas kernels  23.3 us (97%)
  between operations  0.69 us (3%)
    pallas_call x1, Pallas kernels, gathered(): pl.pallas_call(functools.partial(kernel, planes), out_shape=jax.ShapeDtyp...  19.4 us
    pallas_call x1, Pallas kernels, gathered(): pl.pallas_call(multiply, out_shape=(jax.ShapeDtypeStruct((depth, width),...  3.86 us

profile of v6, /device:TPU:1, one launch (start us, length us, event | category | flops | bytes accessed | tf_op | source)
XLA Modules:
  0.0 24.0 jit_solution(12743639622809846393)
XLA Ops:
  0.6 0.0 copy-start.1
  0.6 0.0 copy-start
  0.7 0.0 copy-start.2
  0.7 19.4 %shard_map.59.gram = bf16[4,4,256,256]{3,2,1,0:T(8,128)(2,1)S(1)} custom-call(bf16[256,128]{1,0:T(8,128)(2,1)} %sigma_ref.1), custom_call_target="tpu_custom_call" | custom-call | bytes 16777216 | tf_op jit(solution)/shard_map/pallas_call | solution.py:242
  20.1 0.0 copy-done.1
  20.1 0.0 copy-done
  20.1 0.0 copy-done.2
  20.1 3.9 %shard_map.60 = (bf16[1024,1024]{1,0:T(8,128)(2,1)}, f32[1,1024]{1,0:T(1,128)}) custom-call(s32[1,4]{1,0:T(1,128)S(1)} %copy-done.2, bf16[4,4,256,256]{3,2,1,0:T(8,128)(2,1)S(1)} %shard_map.59.gram, bf16[1024,1024]{1,0:T(8,128)(2,1)S(1)} %bitcast.2, f32[1,1024]{1,0:T(1,128)S(1)} %copy-done.1), custom_call_target="tpu_custom_call" | custom-call | flops 2147483648 | bytes 4194304 | tf_op jit(solution)/shard_map/pallas_call | solution.py:262
Async XLA Ops:
  0.6 19.5 %copy-start.1 = (f32[1,1024]{1,0:T(1,128)S(1)}, f32[1,1024]{1,0:T(1,128)}, u32[]{:S(2)}) copy-start(f32[1,1024]{1,0:T(1,128)} %diag_ref.1) | copy-start | bytes 12292
  0.6 19.5 %copy-start = (bf16[1,1024,1024]{2,1,0:T(8,128)(2,1)S(1)}, bf16[1,1024,1024]{2,1,0:T(8,128)(2,1)}, u32[]{:S(2)}) copy-start(bf16[1,1024,1024]{2,1,0:T(8,128)(2,1)} %param.6) | copy-start | bytes 6291460
  0.7 19.5 %copy-start.2 = (s32[1,4]{1,0:T(1,128)S(1)}, s32[1,4]{1,0:T(1,128)}, u32[]{:S(2)}) copy-start(s32[1,4]{1,0:T(1,128)} %structure_ref.1) | copy-start | bytes 52
